TPU v7x, 512 devices: a whole 4x8x8 slice. The times are simulated.
512 devices in a mesh: dp: 32 (over x, y), seq: 16 (over z, core).
Axes of the slice: x: 4, y: 8, z: 8, core: 2. Of those that a mesh axis runs over, the one named last changes fastest.
Arguments:
- encoder_timesteps: bfloat16 [8192, 16, 1536], P(('dp', 'seq')), may hold values from -10 to 10
- tile_parent_sequence: int32 [8192], P(('dp', 'seq')), may hold values from 0 to 15, as said below
- tile_recording_label: int32 [8192], P(('dp', 'seq')), may hold values from 0 to 3
- tile_valid_timesteps: int32 [8192], P(('dp', 'seq')), may hold values from 1 to 16, as said below
- standardize_scaling: float32 [1536], replicated, may hold values from 0.5 to 1.5
- triple_projector: bfloat16 [1536, 2304], P('dp'), may hold values from -0.15625 to 0.15625
- final_projector: bfloat16 [768, 1536], P('dp'), may hold values from -0.21875 to 0.21875
- lowered_maps: bfloat16 [2, 1536, 64], P(None, 'dp'), may hold values from -0.15625 to 0.15625
- raising_maps: bfloat16 [2, 64, 768], P(None, None, 'dp'), may hold values from -0.75 to 0.75
- focus_softness: float32 [8], replicated, may hold values from 2 to 12
- result_adjoint: bfloat16 [8192, 16, 1536], P(('dp', 'seq')), may hold values from -0.015625 to 0.015625
Outputs:
- block_out: bfloat16 [8192, 16, 1536], P(('dp', 'seq'))
- down_gradient: float32 [2, 1536, 64], P(None, 'dp')
- up_gradient: float32 [2, 64, 768], P(None, None, 'dp')
Inputs may be any that keep to these rules, and one draw needn't show every extreme that they name: `tile_parent_sequence`: at most 2 panels of one device go to one owner, and in every dp group one owner receives exactly 2 panels from every device of the group. `tile_valid_timesteps`: A clip is the set of panels of one dp group with the same tile_parent_sequence and tile_recording_label; every panel of a clip holds 16 frames except the clip's last panel in order of panel index.
All inputs are finite; a program needn't handle non-finite values.
Results may differ from a plain program's by a relative error of at most 0.028.
Values may be sent and summed in bfloat16 or wider, within the bound.
No kernel may reach another device: no remote copies, remote signals or barrier semaphores. Data moves between devices by JAX's collectives and lax.ppermute only.
A program may use at most 128 MiB of HBM per device.

v0:
```python
import math

import jax
import jax.numpy as jnp
from jax import lax
from jax.experimental import pallas as pl
from jax.experimental.pallas import tpu as pltpu
from jax.sharding import PartitionSpec as P

EPS_NORM = 1e-05
EPS_HEAD = 1e-06
WIDE = 1536
PANELS = 16
LEN = 16
ROWS = PANELS * LEN
OWNERS = 16
SLOTS = 2
PACKED = OWNERS * SLOTS * LEN
HEAD = 96
FOCI = 4
HALF = FOCI * HEAD
RANK = 64
SHARDS = 32
BLOCK = WIDE // SHARDS
UPS = 2 * HALF // SHARDS
GRAD = 2 * UPS
HIDDEN = 2 * HALF
QUARTER = WIDE // 4
FACTS = 128
QKVL = 3 * HALF + 2 * RANK
F32 = jnp.float32
BF16 = jnp.bfloat16
SMEM = pltpu.MemorySpace.SMEM
VMEM = pltpu.MemorySpace.VMEM


def dot(a, b):
    return lax.dot_general(a, b, (((1,), (0,)), ((), ())), preferred_element_type=F32)


def dot_nt(a, b):
    return lax.dot_general(a, b, (((1,), (1,)), ((), ())), preferred_element_type=F32)


def slot_places(owner_ref):
    owners = [owner_ref[p] for p in range(PANELS)]
    places = []
    for p in range(PANELS):
        rank = jnp.int32(0)
        for q in range(p):
            rank = rank + jnp.where(owners[q] == owners[p], 1, 0)
        places.append(owners[p] * SLOTS + rank)
    return places


def spread(scalars, shape, axis):
    index = lax.broadcasted_iota(jnp.int32, shape, axis)
    panel = index // LEN
    values = jnp.zeros(shape, jnp.int32)
    for p in range(PANELS):
        values = jnp.where(panel == p, scalars[p], values)
    return values, index % LEN


def pack_kernel(owner_ref, tag_ref, live_ref, x_ref, gain_ref, packed_ref):
    place, step = spread(slot_places(owner_ref), (1, ROWS), 1)
    target = place * LEN + step
    slots = lax.broadcasted_iota(jnp.int32, (PACKED, ROWS), 0)
    select = jnp.where(slots == target, 1.0, 0.0).astype(BF16)
    values = x_ref[...].astype(F32)
    centred = values - jnp.mean(values, axis=-1, keepdims=True)
    scaled = centred * lax.rsqrt(jnp.mean(centred * centred, axis=-1, keepdims=True) + EPS_NORM)
    normed = (scaled * gain_ref[...]).astype(BF16)
    packed_ref[:, :, :WIDE] = dot(select, normed).astype(BF16).reshape(OWNERS, SLOTS * LEN, WIDE)
    tags, step = spread([tag_ref[p] for p in range(PANELS)], (ROWS, FACTS), 0)
    lives, _ = spread([live_ref[p] for p in range(PANELS)], (ROWS, FACTS), 0)
    lane = lax.broadcasted_iota(jnp.int32, (ROWS, FACTS), 1)
    alive = jnp.where(step < lives, 1, 0)
    facts = jnp.where(lane == 0, tags, jnp.where(lane == 1, alive, 0)).astype(F32).astype(BF16)
    packed_ref[:, :, WIDE:] = dot(select, facts).astype(BF16).reshape(OWNERS, SLOTS * LEN, FACTS)


def pack(owners, tags, lives, x, gain):
    return pl.pallas_call(
        pack_kernel,
        out_shape=jax.ShapeDtypeStruct((OWNERS, SLOTS * LEN, WIDE + FACTS), BF16),
        in_specs=[pl.BlockSpec(memory_space=SMEM)] * 3 + [pl.BlockSpec(memory_space=VMEM)] * 2,
        out_specs=pl.BlockSpec(memory_space=VMEM),
        compiler_params=pltpu.CompilerParams(vmem_limit_bytes=32 << 20),
        cost_estimate=pl.CostEstimate(
            flops=2 * PACKED * ROWS * WIDE, bytes_accessed=4 * PACKED * WIDE, transcendentals=0
        ),
        name="pack",
    )(owners, tags, lives, x, gain)


def shard_kernel(core_ref, triple_ref, lowered_ref, raising_ref, final_ref, shard_ref):
    core = core_ref[0]
    for n in range(3):
        first = pl.multiple_of(n * HIDDEN + core * HALF, HALF)
        shard_ref[:, n * HALF : (n + 1) * HALF] = triple_ref[:, pl.ds(first, HALF)]
    lowered = [lowered_ref[n].astype(F32) for n in range(2)]
    shard_ref[:, 3 * HALF : QKVL] = jnp.concatenate(lowered, axis=1).astype(BF16)
    raising = jnp.concatenate([raising_ref[n].astype(F32) for n in range(2)], axis=1)
    shard_ref[:, QKVL : QKVL + 2 * RANK] = pad_rows(raising, BLOCK).astype(BF16)
    quarters = []
    for q in range(2):
        first = pl.multiple_of(core * (WIDE // 2) + q * QUARTER, QUARTER)
        quarters.append(final_ref[:, pl.ds(first, QUARTER)].astype(F32))
    shard_ref[:, QKVL + 2 * RANK :] = jnp.concatenate(quarters, axis=0).astype(BF16)


def make_shard(core, triple, lowered, raising, final):
    return pl.pallas_call(
        shard_kernel,
        out_shape=jax.ShapeDtypeStruct((BLOCK, QKVL + 2 * RANK + QUARTER), BF16),
        in_specs=[pl.BlockSpec(memory_space=SMEM)] + [pl.BlockSpec(memory_space=VMEM)] * 4,
        out_specs=pl.BlockSpec(memory_space=VMEM),
        compiler_params=pltpu.CompilerParams(vmem_limit_bytes=60 << 20),
        name="make_shard",
    )(core, triple, lowered, raising, final)


def pack_masked_kernel(owner_ref, live_ref, adjoint_ref, packed_ref):
    place, step = spread(slot_places(owner_ref), (1, ROWS), 1)
    target = place * LEN + step
    slots = lax.broadcasted_iota(jnp.int32, (PACKED, ROWS), 0)
    select = jnp.where(slots == target, 1.0, 0.0).astype(BF16)
    lives, step = spread([live_ref[p] for p in range(PANELS)], (ROWS, 1), 0)
    masked = jnp.where(step < lives, adjoint_ref[...].astype(F32), 0.0).astype(BF16)
    packed_ref[...] = dot(select, masked).astype(BF16).reshape(packed_ref.shape)


def pack_masked(owners, lives, adjoint):
    return pl.pallas_call(
        pack_masked_kernel,
        out_shape=jax.ShapeDtypeStruct((OWNERS, SLOTS * LEN, WIDE), BF16),
        in_specs=[pl.BlockSpec(memory_space=SMEM)] * 2 + [pl.BlockSpec(memory_space=VMEM)],
        out_specs=pl.BlockSpec(memory_space=VMEM),
        compiler_params=pltpu.CompilerParams(vmem_limit_bytes=32 << 20),
        cost_estimate=pl.CostEstimate(
            flops=2 * PACKED * ROWS * WIDE, bytes_accessed=4 * PACKED * WIDE, transcendentals=0
        ),
        name="pack_masked",
    )(owners, lives, adjoint)


def pad_rows(values, rows=128):
    return jnp.concatenate([values, jnp.zeros((rows - values.shape[0], values.shape[1]), values.dtype)], axis=0)


def owner_copies(sources, landing, sems):
    return [pltpu.make_async_copy(source, landing.at[o], sems.at[o]) for o, source in enumerate(sources)]


def raising_of(raise_s):
    tall = raise_s[...].astype(F32).reshape(SHARDS // 2, BLOCK, 2 * RANK)[:, :UPS]
    raising = tall.reshape(HALF, 2 * RANK).T
    row = lax.broadcasted_iota(jnp.int32, raising.shape, 0)
    raise_q = jnp.where(row < RANK, raising, 0.0).astype(BF16)
    raise_v = jnp.where(row < RANK, 0.0, raising).astype(BF16)
    return raise_q, raise_v


def unit(values):
    scale = lax.rsqrt(jnp.sum(values * values, axis=0, keepdims=True) * (1.0 / HEAD) + EPS_HEAD)
    return values * scale, scale


def forward_kernel(
    core_ref,
    soft_ref,
    mine_ref,
    other_ref,
    whole_ref,
    context_ref,
    out_ref,
    weights_ref,
    qkv_ref,
    low_ref,
    mixed_ref,
    inverse_ref,
    normed_s,
    weight_s,
    raise_s,
    base_s,
    row_sems,
    weight_sems,
    raise_sem,
    out_sem,
):
    owner = pl.program_id(0)
    core = core_ref[0]
    rows = owner_copies((mine_ref, other_ref), normed_s, row_sems)
    outs = pltpu.make_async_copy(
        whole_ref.at[:, pl.ds(QKVL + 2 * RANK, QUARTER)], out_ref, out_sem
    )
    tiles = [
        pltpu.make_async_copy(
            whole_ref.at[:, pl.ds(n * 256, 256)],
            weight_s.at[:, pl.ds(n * 256, 256)],
            weight_sems.at[n],
        )
        for n in range(QKVL // 256)
    ]
    half = pl.ds(pl.multiple_of(core * (WIDE // 2), WIDE // 2), WIDE // 2)
    raises = pltpu.make_async_copy(
        whole_ref.at[half, pl.ds(QKVL, 2 * RANK)], raise_s, raise_sem
    )

    @pl.when(owner == 0)
    def _():
        rows[0].start()
        for tile in tiles:
            tile.start()
        raises.start()
        rows[1].start()
        outs.start()
        rows[0].wait()

    @pl.when(owner == 1)
    def _():
        rows[1].wait()
        outs.wait()

    for n, tile in enumerate(tiles):

        @pl.when(owner == 0)
        def _():
            tile.wait()

        columns = slice(n * 256, (n + 1) * 256)
        base_s[:, columns] = dot(normed_s[owner, :, :WIDE], weight_s[:, columns])

    @pl.when(owner == 0)
    def _():
        raises.wait()

    low = base_s[:, 3 * HALF :].astype(BF16)
    low_ref[...] = low
    raise_q, raise_v = raising_of(raise_s)
    query = (base_s[:, :HALF] + dot(low, raise_q)).astype(BF16).astype(F32).T
    key = base_s[:, HALF : 2 * HALF].astype(BF16).astype(F32).T
    value = (base_s[:, 2 * HALF : 3 * HALF] + dot(low, raise_v)).astype(BF16).astype(F32).T
    qkv_ref[:HALF, :] = query.astype(BF16)
    qkv_ref[HALF : 2 * HALF, :] = key.astype(BF16)
    qkv_ref[2 * HALF :, :] = value.astype(BF16)

    rows_j = lax.broadcasted_iota(jnp.int32, (PACKED, PACKED), 0)
    rows_i = lax.broadcasted_iota(jnp.int32, (PACKED, PACKED), 1)
    facts = normed_s[owner, :, WIDE:].astype(F32)
    codes = jnp.where(facts[:, 1:2] > 0.5, facts[:, 0:1], -1.0)
    allowed = (facts.T[0:1, :] == codes) | (rows_j == rows_i)
    ones_rows = jnp.where(lax.broadcasted_iota(jnp.int32, (32, PACKED), 0) < 2, 1.0, 0.0)

    for h in range(FOCI):
        head = slice(h * HEAD, (h + 1) * HEAD)
        temper = soft_ref[core * FOCI + h] * (1.0 / HEAD)
        qn, _ = unit(query[head, :])
        kn, _ = unit(key[head, :])
        qs = pad_rows(qn * (temper * math.log2(math.e))).astype(BF16)
        v = jnp.concatenate([value[head, :], ones_rows], axis=0)
        scores = dot(pad_rows(kn).T.astype(BF16), qs)
        unnormed = jnp.exp2(jnp.where(allowed, scores, -1e30)).astype(BF16)
        weights_ref[h] = unnormed
        mixed = dot(v.astype(BF16), unnormed)
        inverse = 1.0 / mixed[HEAD : HEAD + 1, :]
        inverse_ref[h : h + 1, :] = inverse
        mixed_ref[head, :] = mixed[:HEAD, :] * inverse

    context_ref[...] = mixed_ref[...].T.astype(BF16).reshape(context_ref.shape)


def forward(core, soft, mine, other, whole):
    anywhere = pl.BlockSpec(memory_space=pl.ANY)
    grid = pltpu.PrefetchScalarGridSpec(
        num_scalar_prefetch=1,
        grid=(2,),
        in_specs=[
            pl.BlockSpec(memory_space=SMEM),
        ]
        + [anywhere] * 3,
        out_specs=[
            pl.BlockSpec((OWNERS, None, SLOTS * LEN, HALF), lambda o, c: (0, o, 0, 0)),
            pl.BlockSpec((WIDE, QUARTER), lambda o, c: (0, 0)),
            pl.BlockSpec((None, FOCI, PACKED, PACKED), lambda o, c: (o, 0, 0, 0)),
            pl.BlockSpec((None, 3 * HALF, PACKED), lambda o, c: (o, 0, 0)),
            pl.BlockSpec((None, PACKED, 2 * RANK), lambda o, c: (o, 0, 0)),
            pl.BlockSpec((None, HALF, PACKED), lambda o, c: (o, 0, 0)),
            pl.BlockSpec((None, 8, PACKED), lambda o, c: (o, 0, 0)),
        ],
        scratch_shapes=[
            pltpu.VMEM((2, PACKED, WIDE + FACTS), BF16),
            pltpu.VMEM((WIDE, QKVL), BF16),
            pltpu.VMEM((WIDE // 2, 2 * RANK), BF16),
            pltpu.VMEM((PACKED, QKVL), F32),
            pltpu.SemaphoreType.DMA((2,)),
            pltpu.SemaphoreType.DMA((QKVL // 256,)),
            pltpu.SemaphoreType.DMA,
            pltpu.SemaphoreType.DMA,
        ],
    )
    return pl.pallas_call(
        forward_kernel,
        grid_spec=grid,
        out_shape=(
            jax.ShapeDtypeStruct((OWNERS, 2, SLOTS * LEN, HALF), BF16),
            jax.ShapeDtypeStruct((WIDE, QUARTER), BF16),
            jax.ShapeDtypeStruct((2, FOCI, PACKED, PACKED), BF16),
            jax.ShapeDtypeStruct((2, 3 * HALF, PACKED), BF16),
            jax.ShapeDtypeStruct((2, PACKED, 2 * RANK), BF16),
            jax.ShapeDtypeStruct((2, HALF, PACKED), F32),
            jax.ShapeDtypeStruct((2, 8, PACKED), F32),
        ),
        compiler_params=pltpu.CompilerParams(
            vmem_limit_bytes=60 << 20, dimension_semantics=("arbitrary",)
        ),
        cost_estimate=pl.CostEstimate(
            flops=6 << 30, bytes_accessed=16 << 20, transcendentals=2 * FOCI * PACKED * PACKED
        ),
        name="forward",
    )(core, soft, mine, other, whole)


def backward_kernel(
    core_ref,
    soft_ref,
    weights_ref,
    qkv_ref,
    low_ref,
    mixed_ref,
    inverse_ref,
    mine_ref,
    other_ref,
    masked_mine_ref,
    masked_other_ref,
    whole_ref,
    out_own_ref,
    out_other_ref,
    keep_ref,
    send_ref,
    up_ref,
    normed_s,
    masked_s,
    out_s,
    tight_s,
    raise_s,
    cot_s,
    dquery_s,
    dvalue_s,
    down_s,
    up_s,
    row_sems,
    masked_sems,
    out_sems,
    raise_sem,
):
    owner = pl.program_id(0)
    core = core_ref[0]
    body = pl.ds(0, WIDE)
    rows = owner_copies((mine_ref.at[:, body], other_ref.at[:, body]), normed_s, row_sems)
    masks = owner_copies((masked_mine_ref, masked_other_ref), masked_s, masked_sems)
    half = pl.ds(pl.multiple_of(core * (WIDE // 2), WIDE // 2), WIDE // 2)
    raises = pltpu.make_async_copy(
        whole_ref.at[half, pl.ds(QKVL, 2 * RANK)], raise_s, raise_sem
    )
    outs = owner_copies(
        (out_own_ref.at[half, :], out_other_ref.at[half, :]),
        out_s,
        out_sems,
    )

    @pl.when(owner == 0)
    def _():
        masks[0].start()
        outs[0].start()
        outs[1].start()
        rows[0].start()
        raises.start()
        masks[1].start()
        rows[1].start()
        down_s[...] = jnp.zeros_like(down_s)
        up_s[...] = jnp.zeros_like(up_s)
        masks[0].wait()
        for n, out in enumerate(outs):
            out.wait()
            tall = out_s[n].astype(F32).reshape(SHARDS // 2, BLOCK, QUARTER)
            for q in range(2):
                tight = tall[:, q * UPS : (q + 1) * UPS].reshape(HALF, QUARTER)
                tight_s[n, :, q * QUARTER : (q + 1) * QUARTER] = tight.astype(BF16)

    @pl.when(owner == 1)
    def _():
        masks[1].wait()

    total = jnp.zeros((HALF, PACKED), F32)
    for n, side in enumerate((core, 1 - core)):
        columns = pl.ds(pl.multiple_of(side * (WIDE // 2), WIDE // 2), WIDE // 2)
        total = total + dot_nt(tight_s[n], masked_s[owner, :, columns])
    cot_s[...] = total.astype(BF16).astype(F32)

    ones_rows = jnp.where(lax.broadcasted_iota(jnp.int32, (32, PACKED), 0) < 2, 1.0, 0.0)
    sub = lax.broadcasted_iota(jnp.int32, (32, PACKED), 0)

    for h in range(FOCI):
        head = slice(h * HEAD, (h + 1) * HEAD)
        temper = soft_ref[core * FOCI + h] * (1.0 / HEAD)
        qn, rq = unit(qkv_ref[head, :].astype(F32))
        kn, _ = unit(qkv_ref[HALF + h * HEAD : HALF + (h + 1) * HEAD, :].astype(F32))
        value = qkv_ref[2 * HALF + h * HEAD : 2 * HALF + (h + 1) * HEAD, :].astype(F32)
        v = jnp.concatenate([value, ones_rows], axis=0)
        unnormed = weights_ref[h]
        dc = (cot_s[head, :] * inverse_ref[h : h + 1, :]).astype(BF16)
        shift = jnp.sum(dc.astype(F32) * mixed_ref[head, :], axis=0, keepdims=True)
        shift_top = shift.astype(BF16).astype(F32)
        extra = jnp.where(sub == 0, -shift_top, jnp.where(sub == 1, shift_top - shift, 0.0))
        dc = jnp.concatenate([dc, extra.astype(BF16)], axis=0)
        inner = dot(v.T.astype(BF16), dc)
        dscores = (unnormed.astype(F32) * inner).astype(BF16)
        dqn = dot(pad_rows(kn).astype(BF16), dscores)[:HEAD, :] * temper
        dq = rq * (dqn - qn * (jnp.sum(qn * dqn, axis=0, keepdims=True) * (1.0 / HEAD)))
        dquery_s[head, :] = dq.astype(BF16)
        dv = dot_nt(unnormed, dc)
        dvalue_s[head, :] = dv.T[:HEAD, :].astype(BF16)

    @pl.when(owner == 0)
    def _():
        raises.wait()
        rows[0].wait()

    @pl.when(owner == 1)
    def _():
        rows[1].wait()

    low = low_ref[...]
    raise_q, raise_v = raising_of(raise_s)
    dquery = dquery_s[...]
    dvalue = dvalue_s[...]
    lane = lax.broadcasted_iota(jnp.int32, (HALF, 2 * RANK), 1)
    up_s[...] += jnp.where(lane < RANK, dot(dquery, low), dot(dvalue, low))
    inner_t = (dot(raise_q, dquery) + dot(raise_v, dvalue)).astype(BF16)
    down_s[...] += dot(inner_t, normed_s[owner])

    @pl.when(owner == 1)
    def _():
        down = down_s[...].T.reshape(SHARDS, BLOCK, 2 * RANK)
        first = down[:, :UPS].reshape(SHARDS * UPS, 2 * RANK)
        second = down[:, UPS:].reshape(SHARDS * UPS, 2 * RANK)
        keep_ref[...] = jnp.where(core == 0, first, second)
        send_ref[...] = jnp.where(core == 0, second, first).astype(BF16)
        up_ref[...] = up_s[...]


def backward(core, soft, saved, normed, masked, whole, out_own, out_other):
    anywhere = pl.BlockSpec(memory_space=pl.ANY)
    grid = pltpu.PrefetchScalarGridSpec(
        num_scalar_prefetch=1,
        grid=(2,),
        in_specs=[
            pl.BlockSpec(memory_space=SMEM),
            pl.BlockSpec((None, FOCI, PACKED, PACKED), lambda o, c: (o, 0, 0, 0)),
            pl.BlockSpec((None, 3 * HALF, PACKED), lambda o, c: (o, 0, 0)),
            pl.BlockSpec((None, PACKED, 2 * RANK), lambda o, c: (o, 0, 0)),
            pl.BlockSpec((None, HALF, PACKED), lambda o, c: (o, 0, 0)),
            pl.BlockSpec((None, 8, PACKED), lambda o, c: (o, 0, 0)),
        ]
        + [anywhere] * 7,
        out_specs=[
            pl.BlockSpec((SHARDS * UPS, 2 * RANK), lambda o, c: (0, 0)),
            pl.BlockSpec((SHARDS * UPS, 2 * RANK), lambda o, c: (0, 0)),
            pl.BlockSpec((HALF, 2 * RANK), lambda o, c: (0, 0)),
        ],
        scratch_shapes=[
            pltpu.VMEM((2, PACKED, WIDE), BF16),
            pltpu.VMEM((2, PACKED, WIDE), BF16),
            pltpu.VMEM((2, WIDE // 2, QUARTER), BF16),
            pltpu.VMEM((2, HALF, WIDE // 2), BF16),
            pltpu.VMEM((WIDE // 2, 2 * RANK), BF16),
            pltpu.VMEM((HALF, PACKED), F32),
            pltpu.VMEM((HALF, PACKED), BF16),
            pltpu.VMEM((HALF, PACKED), BF16),
            pltpu.VMEM((2 * RANK, WIDE), F32),
            pltpu.VMEM((HALF, 2 * RANK), F32),
            pltpu.SemaphoreType.DMA((2,)),
            pltpu.SemaphoreType.DMA((2,)),
            pltpu.SemaphoreType.DMA((2,)),
            pltpu.SemaphoreType.DMA,
        ],
    )
    return pl.pallas_call(
        backward_kernel,
        grid_spec=grid,
        out_shape=(
            jax.ShapeDtypeStruct((SHARDS * UPS, 2 * RANK), F32),
            jax.ShapeDtypeStruct((SHARDS * UPS, 2 * RANK), BF16),
            jax.ShapeDtypeStruct((HALF, 2 * RANK), F32),
        ),
        compiler_params=pltpu.CompilerParams(
            vmem_limit_bytes=48 << 20, dimension_semantics=("arbitrary",)
        ),
        cost_estimate=pl.CostEstimate(flops=8 << 30, bytes_accessed=16 << 20, transcendentals=0),
        name="backward",
    )(core, soft, *saved, *normed, *masked, whole, out_own, out_other)


def combine_kernel(core_ref, keep_ref, come_ref, up_ref, parts_ref):
    down = keep_ref[...] + come_ref[...].astype(F32)
    up = up_ref[...]
    none = jnp.zeros_like(up)
    low_half = core_ref[0] == 0
    up = jnp.concatenate([jnp.where(low_half, up, none), jnp.where(low_half, none, up)], axis=0)
    shape = (SHARDS, UPS, 2 * RANK)
    parts = jnp.concatenate([down.reshape(shape), up.reshape(shape)], axis=1)
    parts_ref[...] = parts.reshape(parts_ref.shape).astype(BF16)


def combine(core, keep, come, up):
    return pl.pallas_call(
        combine_kernel,
        out_shape=jax.ShapeDtypeStruct((SHARDS * GRAD, 2 * RANK), BF16),
        in_specs=[pl.BlockSpec(memory_space=SMEM)] + [pl.BlockSpec(memory_space=VMEM)] * 3,
        out_specs=pl.BlockSpec(memory_space=VMEM),
        compiler_params=pltpu.CompilerParams(vmem_limit_bytes=8 << 20),
        name="combine",
    )(core, keep, come, up)


def finish_kernel(core_ref, owner_ref, live_ref, context_ref, x_ref, *refs):
    *out_refs, block_ref = refs
    core = core_ref[0]
    place, step = spread(slot_places(owner_ref), (ROWS, 1), 0)
    target = place * LEN + step
    slots = lax.broadcasted_iota(jnp.int32, (ROWS, PACKED), 1)
    select = jnp.where(slots == target, 1.0, 0.0).astype(BF16)
    lives, _ = spread([live_ref[p] for p in range(PANELS)], (ROWS, 1), 0)
    halves = []
    for half in range(2):
        parts = []
        for o in range(OWNERS):
            source = o // 2 * 2 + half
            first = 0 if source == o else SLOTS * LEN
            parts.append(context_ref[source, first : first + SLOTS * LEN, :])
        halves.append(dot(select, jnp.concatenate(parts, axis=0)).astype(BF16))
    for n, ref in enumerate(out_refs):
        side = core if n < 2 else 1 - core
        first = pl.multiple_of(side * (WIDE // 2) + n % 2 * QUARTER, QUARTER)
        columns = pl.ds(first, QUARTER)
        attended = dot(halves[0], ref[:HALF, :]) + dot(halves[1], ref[HALF:, :])
        added = jnp.where(step < lives, attended, 0.0)
        block_ref[:, columns] = (x_ref[:, columns].astype(F32) + added).astype(BF16)


def finish(core, owners, lives, context, x, outs):
    return pl.pallas_call(
        finish_kernel,
        out_shape=jax.ShapeDtypeStruct((ROWS, WIDE), BF16),
        in_specs=[pl.BlockSpec(memory_space=SMEM)] * 3 + [pl.BlockSpec(memory_space=VMEM)] * 6,
        out_specs=pl.BlockSpec(memory_space=VMEM),
        compiler_params=pltpu.CompilerParams(vmem_limit_bytes=40 << 20),
        cost_estimate=pl.CostEstimate(
            flops=2 * ROWS * 2 * HALF * (WIDE + PACKED), bytes_accessed=6 << 20, transcendentals=0
        ),
        name="finish",
    )(core, owners, lives, context, x, *outs)


def add_shards_kernel(part_ref, total_ref):
    total = part_ref[0].astype(F32)
    for t in range(1, SHARDS):
        total = total + part_ref[t].astype(F32)
    total = total.astype(BF16)
    for o in range(OWNERS):
        total_ref[o] = total


def add_shards(parts):
    return pl.pallas_call(
        add_shards_kernel,
        out_shape=jax.ShapeDtypeStruct((OWNERS, GRAD, 2 * RANK), BF16),
        in_specs=[pl.BlockSpec(memory_space=VMEM)],
        out_specs=pl.BlockSpec(memory_space=VMEM),
        compiler_params=pltpu.CompilerParams(vmem_limit_bytes=8 << 20),
        name="add_shards",
    )(parts)


def add_owners_kernel(part_ref, down_ref, up_ref):
    downs = [jnp.zeros((UPS, 2 * RANK), F32)] * 2
    up = jnp.zeros((UPS, 2 * RANK), F32)
    for o in range(OWNERS):
        part = part_ref[o].astype(F32)
        downs[o % 2] = downs[o % 2] + part[:UPS, :]
        up = up + part[UPS:, :]
    down = jnp.concatenate(downs, axis=0)
    for n in range(2):
        down_ref[n] = down[:, n * RANK : (n + 1) * RANK]
        up_ref[n] = up[:, n * RANK : (n + 1) * RANK]


def add_owners(parts):
    return pl.pallas_call(
        add_owners_kernel,
        out_shape=(
            jax.ShapeDtypeStruct((2, BLOCK, RANK), F32),
            jax.ShapeDtypeStruct((2, UPS, RANK), F32),
        ),
        in_specs=[pl.BlockSpec(memory_space=VMEM)],
        out_specs=(pl.BlockSpec(memory_space=VMEM),) * 2,
        compiler_params=pltpu.CompilerParams(vmem_limit_bytes=8 << 20),
        name="add_owners",
    )(parts)


def exchange(data, axis):
    return lax.all_to_all(data, axis, split_axis=0, concat_axis=0, tiled=True)


def swap_cores(data):
    pairs = [(s, s ^ 1) for s in range(OWNERS)]
    return lax.ppermute(data, "seq", pairs)


def on_device(
    encoder_timesteps,
    tile_parent_sequence,
    tile_recording_label,
    tile_valid_timesteps,
    standardize_scaling,
    triple_projector,
    final_projector,
    lowered_maps,
    raising_maps,
    focus_softness,
    result_adjoint,
):
    core = (lax.axis_index("seq") % 2).astype(jnp.int32).reshape(1)
    shard = make_shard(
        core, triple_projector, lowered_maps, jnp.swapaxes(raising_maps, 1, 2), final_projector
    )
    whole = lax.all_gather(shard, "dp", axis=0, tiled=True)

    x = encoder_timesteps.reshape(ROWS, WIDE)
    packed = pack(
        tile_parent_sequence,
        tile_recording_label,
        tile_valid_timesteps,
        x,
        standardize_scaling.reshape(1, WIDE),
    )
    packed, adjoint = lax.optimization_barrier((packed, result_adjoint.reshape(ROWS, WIDE)))
    masked = pack_masked(tile_parent_sequence, tile_valid_timesteps, adjoint)
    packed = exchange(packed, "seq")
    packed, masked = lax.optimization_barrier((packed, masked))
    masked = exchange(masked, "seq")
    normed = [part.reshape(PACKED, WIDE + FACTS) for part in (packed, swap_cores(packed))]
    context, out_own, *saved = forward(core, focus_softness, *normed, whole)
    masked, context = lax.optimization_barrier((masked, context))
    masked = [part.reshape(PACKED, WIDE) for part in (masked, swap_cores(masked))]
    out_other = swap_cores(out_own)
    keep, send, up = backward(core, focus_softness, saved, normed, masked, whole, out_own, out_other)
    context = exchange(context.reshape(OWNERS, 2 * SLOTS * LEN, HALF), "seq")
    parts = combine(core, keep, swap_cores(send), up)
    outs = []
    for part in (out_own, out_other):
        part = part.reshape(SHARDS, BLOCK, QUARTER)
        outs += [part[:, :UPS].reshape(HIDDEN, QUARTER), part[:, UPS:].reshape(HIDDEN, QUARTER)]
    parts, context = lax.optimization_barrier((parts, context))
    parts = exchange(parts.reshape(SHARDS, GRAD, 2 * RANK), "dp")
    block_out = finish(core, tile_parent_sequence, tile_valid_timesteps, context, x, outs)
    shard_down, shard_up = add_owners(exchange(add_shards(parts), "seq"))
    return block_out.reshape(encoder_timesteps.shape), shard_down, jnp.swapaxes(shard_up, 1, 2)


def solution(mesh):
    in_specs = (
        P(("dp", "seq"), None, None),
        P(("dp", "seq")),
        P(("dp", "seq")),
        P(("dp", "seq")),
        P(),
        P("dp", None),
        P("dp", None),
        P(None, "dp", None),
        P(None, None, "dp"),
        P(),
        P(("dp", "seq"), None, None),
    )
    out_specs = (P(("dp", "seq"), None, None), P(None, "dp", None), P(None, None, "dp"))
    return jax.shard_map(
        on_device, mesh=mesh, in_specs=in_specs, out_specs=out_specs, check_vma=False
    )
```

profile of v0, /device:TPU:1, one launch (start us, length us, event | category | flops | bytes accessed | tf_op | source)
XLA Modules:
  0.0 204.7 jit_solution(12130222390215472880)
XLA Ops:
  7.2 1.8 make_shard.1
  9.7 1.1 copy-done
  12.8 2.9 %pack.1 = bf16[16,32,1664]{2,1,0:T(8,128)(2,1)} custom-call(s32[16]{0:T(128)S(1)} %copy-done.4, s32[16]{0:T(128)S(1)} %copy-done.8, s32[16]{0:T(128)S(1)} %copy-done.6, bf16[256,1536]{1,0:T(8,128)(2,1)S(1)} %bitcast.18, f32[1,1536]{1,0:T(1,128)S(1)} %reshape.59.gain_ref), custom_call_target="tpu_custom_call" | custom-call | flops 402653184 | bytes 3145728 | tf_op jit(solution)/shard_map/pack/pallas_call | solution.py:84
  15.7 12.0 %all-to-all-start = ((bf16[16,32,1664]{2,1,0:T(8,128)(2,1)}), bf16[16,32,1664]{2,1,0:T(8,128)(2,1)S(1)}, u32[]{:S(2)}, u32[]{:S(2)}) async-start(bf16[16,32,1664]{2,1,0:T(8,128)(2,1)} %pack.1), calls=%async_computation | async-start | bytes 3407872 | tf_op jit(solution)/shard_map/all_to_all | solution.py:615
  27.7 2.4 %pack_masked.1 = bf16[16,32,1536]{2,1,0:T(8,128)(2,1)} custom-call(s32[16]{0:T(128)S(1)} %copy-done.5, s32[16]{0:T(128)S(1)} %copy-done.7, bf16[256,1536]{1,0:T(8,128)(2,1)S(1)} %bitcast.27), custom_call_target="tpu_custom_call" | custom-call | flops 402653184 | bytes 3145728 | tf_op jit(solution)/shard_map/pack_masked/pallas_call | solution.py:135
  30.1 38.6 %all-to-all-done = bf16[16,32,1664]{2,1,0:T(8,128)(2,1)S(1)} async-done(((bf16[16,32,1664]{2,1,0:T(8,128)(2,1)}), bf16[16,32,1664]{2,1,0:T(8,128)(2,1)S(1)}, u32[]{:S(2)}, u32[]{:S(2)}) %all-to-all-start) | async-done | bytes 1703968 | tf_op jit(solution)/shard_map/all_to_all | solution.py:615
  68.7 4.4 %all-to-all-start.1 = ((bf16[16,32,1536]{2,1,0:T(8,128)(2,1)}), bf16[16,32,1536]{2,1,0:T(8,128)(2,1)}, u32[]{:S(2)}, u32[]{:S(2)}) async-start(bf16[16,32,1536]{2,1,0:T(8,128)(2,1)} %pack_masked.1), calls=%async_computation.1 | async-start | bytes 3145728 | tf_op jit(solution)/shard_map/all_to_all | solution.py:615
  73.2 2.1 %collective-permute-start = (bf16[16,32,1664]{2,1,0:T(8,128)(2,1)S(1)}, bf16[16,32,1664]{2,1,0:T(8,128)(2,1)S(1)}, u32[]{:S(2)}, u32[]{:S(2)}) collective-permute-start(bf16[16,32,1664]{2,1,0:T(8,128)(2,1)S(1)} %all-to-all-done), channel_id=1, source_target_pairs={{0,1},{1,0},{2,3},{3,2},{4,5},{5,4},{6,7},{7,6},{8,9},{9,8},{10,11... | collective-permute-start | bytes 5111816 | tf_op jit(solution)/shard_map/ppermute | solution.py:620
  75.3 3.4 %collective-permute-done = bf16[16,32,1664]{2,1,0:T(8,128)(2,1)S(1)} collective-permute-done((bf16[16,32,1664]{2,1,0:T(8,128)(2,1)S(1)}, bf16[16,32,1664]{2,1,0:T(8,128)(2,1)S(1)}, u32[]{:S(2)}, u32[]{:S(2)}) %collective-permute-start) | collective-permute-done | bytes 1703968 | tf_op jit(solution)/shard_map/ppermute | solution.py:620
  78.7 27.7 %all-gather.2.cloned.1.call-done.whole_ref = bf16[1536,1792]{1,0:T(8,128)(2,1)} async-done(((bf16[48,1792]{1,0:T(8,128)(2,1)}), bf16[1536,1792]{1,0:T(8,128)(2,1)}) %all-gather.2.cloned.1.call-update) | async-done | bytes 5505040 | tf_op jit(solution)/shard_map/all_gather | solution.py:640
  106.4 19.3 %forward.1 = (bf16[16,2,32,384]{3,2,1,0:T(8,128)(2,1)}, bf16[1536,384]{1,0:T(8,128)(2,1)}, bf16[2,4,512,512]{3,2,1,0:T(8,128)(2,1)}, bf16[2,1152,512]{2,1,0:T(8,...) custom-call(s32[1]{0:T(128)} %bitcast.core_ref, f32[8]{0:T(128)} %soft_ref.3, ...), custom_call_target="tpu_custom_call" | custom-call | flops 6442450944 | bytes 16777216 | tf_op jit(solution)/shard_map/forward/pallas_call | solution.py:303
  125.8 4.8 %collective-permute-start.1 = (bf16[16,32,1536]{2,1,0:T(8,128)(2,1)}, bf16[16,32,1536]{2,1,0:T(8,128)(2,1)}, u32[]{:S(2)}, u32[]{:S(2)}) collective-permute-start(bf16[16,32,1536]{2,1,0:T(8,128)(2,1)} %all-to-all-done.1), channel_id=1, source_target_pairs={{0,1},{1,0},{2,3},{3,2},{4,5},{5,4},{6,7},{7,6},{8,9},{9,8},{10,11... | collective-permute-start | bytes 4718600 | tf_op jit(solution)/shard_map/ppermute | solution.py:620
  130.6 1.9 collective-permute-start.2
  132.5 7.9 %all-to-all-start.2 = ((bf16[16,64,384]{2,1,0:T(8,128)(2,1)}), bf16[16,64,384]{2,1,0:T(8,128)(2,1)S(1)}, u32[]{:S(2)}, u32[]{:S(2)}) async-start(bf16[16,64,384]{2,1,0:T(8,128)(2,1)} %bitcast.30), calls=%async_computation.2 | async-start | bytes 1572864 | tf_op jit(solution)/shard_map/all_to_all | solution.py:615
  140.5 1.4 copy-done.10
  142.8 11.3 %backward.1 = (f32[768,128]{1,0:T(8,128)S(1)}, bf16[768,128]{1,0:T(8,128)(2,1)S(1)}, f32[384,128]{1,0:T(8,128)S(1)}) custom-call(s32[1]{0:T(128)} %bitcast.core_ref, f32[8]{0:T(128)S(1)} %copy-done.9, bf16[2,4,512,512]{3,2,1,0:T(8,128)(2,1)} %get-tuple-element.26.weights_ref, bf16[2,1152,512]{2,1,0:T(8,128)(2,1)} %get-tuple-element.27.qkv_ref, ...), custom_call_target="tpu_custom_call" | custom-call | flops 8589934592 | bytes 16777216 | tf_op jit(solution)/shard_map/backward/pallas_call | solution.py:490
  154.2 2.0 collective-permute-start.3
  156.2 1.3 collective-permute-done.3.come_ref
  157.5 5.5 %all-to-all-done.2.context_ref = bf16[16,64,384]{2,1,0:T(8,128)(2,1)S(1)} async-done(((bf16[16,64,384]{2,1,0:T(8,128)(2,1)}), bf16[16,64,384]{2,1,0:T(8,128)(2,1)S(1)}, u32[]{:S(2)}, u32[]{:S(2)}) %all-to-all-start.2) | async-done | bytes 786464 | tf_op jit(solution)/shard_map/all_to_all | solution.py:615
  163.1 18.4 %all_to_all.25.part_ref = bf16[32,48,128]{2,1,0:T(8,128)(2,1)S(1)} all-to-all(bf16[32,48,128]{2,1,0:T(8,128)(2,1)S(1)} %bitcast.24), channel_id=1, replica_groups=mesh['dp'=32,'seq'=16] {'dp'}, dimensions={0} | all-to-all | bytes 786432 | tf_op jit(solution)/shard_map/all_to_all | solution.py:615
  182.2 4.6 %all-to-all-start.4 = ((bf16[16,48,128]{2,1,0:T(8,128)(2,1)}), bf16[16,48,128]{2,1,0:T(8,128)(2,1)S(1)}, u32[]{:S(2)}, u32[]{:S(2)}) async-start(bf16[16,48,128]{2,1,0:T(8,128)(2,1)} %add_shards.1), calls=%async_computation.4 | async-start | bytes 393216 | tf_op jit(solution)/shard_map/all_to_all | solution.py:615
  187.1 1.0 copy-done.1
  188.1 3.1 %finish.1 = bf16[256,1536]{1,0:T(8,128)(2,1)} custom-call(s32[1]{0:T(128)} %bitcast.core_ref, s32[16]{0:T(128)S(1)} %copy-done.5, s32[16]{0:T(128)S(1)} %copy-done.7, bf16[16,64,384]{2,1,0:T(8,128)(2,1)S(1)} %all-to-all-done.2.context_ref, bf16[256,1536]{1,0:T(8,128)(2,1)S(1)} %bitcast.19, bf16[768,384]{1,0:T(8,128)(2,1)S(1)} %bitcast.21, ...), custom_call_target="tpu_custom_call" | custom-call | flops 805306368 | bytes 6291456 | tf_op jit(solution)/shard_map/finish/pallas_call | solution.py:554
  191.1 6.0 %all-to-all-done.4.part_ref = bf16[16,48,128]{2,1,0:T(8,128)(2,1)S(1)} async-done(((bf16[16,48,128]{2,1,0:T(8,128)(2,1)}), bf16[16,48,128]{2,1,0:T(8,128)(2,1)S(1)}, u32[]{:S(2)}, u32[]{:S(2)}) %all-to-all-start.4) | async-done | bytes 196640 | tf_op jit(solution)/shard_map/all_to_all | solution.py:615
  (38 shorter events, 5.5 us)
Async XLA Ops:
  7.2 99.2 %all-gather.2.cloned.1.call-start = ((), (), s32[]{:S(2)}) async-start(), calls=%async_computation.5 | async-start | bytes 5677056 | tf_op jit(solution)/shard_map/all_gather | solution.py:640
  9.7 1.1 copy-start
  10.9 0.7 copy-start.4
  11.5 0.7 copy-start.6
  12.2 0.7 copy-start.8
  15.7 12.0 %copy-start.3 = (bf16[16,16,1536]{2,1,0:T(8,128)(2,1)S(1)}, bf16[16,16,1536]{2,1,0:T(8,128)(2,1)}, u32[]{:S(2)}) copy-start(bf16[16,16,1536]{2,1,0:T(8,128)(2,1)} %param.21) | copy-start | bytes 2359300
  15.7 12.0 %copy-start.5 = (s32[16]{0:T(128)S(1)}, s32[16]{0:T(128)}, u32[]{:S(2)}) copy-start(s32[16]{0:T(128)} %owner_ref.5) | copy-start | bytes 196
  15.7 12.0 %copy-start.7 = (s32[16]{0:T(128)S(1)}, s32[16]{0:T(128)}, u32[]{:S(2)}) copy-start(s32[16]{0:T(128)} %live_ref.5) | copy-start | bytes 196
  15.7 53.0 %all-to-all-start = ((bf16[16,32,1664]{2,1,0:T(8,128)(2,1)}), bf16[16,32,1664]{2,1,0:T(8,128)(2,1)S(1)}, u32[]{:S(2)}, u32[]{:S(2)}) async-start(bf16[16,32,1664]{2,1,0:T(8,128)(2,1)} %pack.1), calls=%async_computation | async-start | bytes 3407872 | tf_op jit(solution)/shard_map/all_to_all | solution.py:615
  68.7 4.4 %copy-start.13 = (bf16[16,32,1664]{2,1,0:T(8,128)(2,1)}, bf16[16,32,1664]{2,1,0:T(8,128)(2,1)S(1)}, u32[]{:S(2)}) copy-start(bf16[16,32,1664]{2,1,0:T(8,128)(2,1)S(1)} %all-to-all-done) | copy-start | bytes 5111812
  68.7 57.0 %all-to-all-start.1 = ((bf16[16,32,1536]{2,1,0:T(8,128)(2,1)}), bf16[16,32,1536]{2,1,0:T(8,128)(2,1)}, u32[]{:S(2)}, u32[]{:S(2)}) async-start(bf16[16,32,1536]{2,1,0:T(8,128)(2,1)} %pack_masked.1), calls=%async_computation.1 | async-start | bytes 3145728 | tf_op jit(solution)/shard_map/all_to_all | solution.py:615
  73.2 5.5 %collective-permute-start = (bf16[16,32,1664]{2,1,0:T(8,128)(2,1)S(1)}, bf16[16,32,1664]{2,1,0:T(8,128)(2,1)S(1)}, u32[]{:S(2)}, u32[]{:S(2)}) collective-permute-start(bf16[16,32,1664]{2,1,0:T(8,128)(2,1)S(1)} %all-to-all-done), channel_id=1, source_target_pairs={{0,1},{1,0},{2,3},{3,2},{4,5},{5,4},{6,7},{7,6},{8,9},{9,8},{10,11... | collective-permute-start | bytes 5111816 | tf_op jit(solution)/shard_map/ppermute | solution.py:620
  78.7 27.7 %copy-start.14 = (bf16[16,32,1664]{2,1,0:T(8,128)(2,1)}, bf16[16,32,1664]{2,1,0:T(8,128)(2,1)S(1)}, u32[]{:S(2)}) copy-start(bf16[16,32,1664]{2,1,0:T(8,128)(2,1)S(1)} %collective-permute-done) | copy-start | bytes 5111812
  125.7 14.7 %copy-start.2 = (bf16[1536,384]{1,0:T(8,128)(2,1)S(1)}, bf16[1536,384]{1,0:T(8,128)(2,1)}, u32[]{:S(2)}) copy-start(bf16[1536,384]{1,0:T(8,128)(2,1)} %get-tuple-element.34.out_own_ref) | copy-start | bytes 3538948
  125.7 14.7 %copy-start.9 = (f32[8]{0:T(128)S(1)}, f32[8]{0:T(128)}, u32[]{:S(2)}) copy-start(f32[8]{0:T(128)} %soft_ref.3) | copy-start | bytes 100
  125.8 14.7 %copy-start.12 = (f32[2,8,512]{2,1,0:T(8,128)S(1)}, f32[2,8,512]{2,1,0:T(8,128)}, u32[]{:S(2)}) copy-start(f32[2,8,512]{2,1,0:T(8,128)} %get-tuple-element.30.inverse_ref) | copy-start | bytes 98308
  125.8 14.6 %collective-permute-start.1 = (bf16[16,32,1536]{2,1,0:T(8,128)(2,1)}, bf16[16,32,1536]{2,1,0:T(8,128)(2,1)}, u32[]{:S(2)}, u32[]{:S(2)}) collective-permute-start(bf16[16,32,1536]{2,1,0:T(8,128)(2,1)} %all-to-all-done.1), channel_id=1, source_target_pairs={{0,1},{1,0},{2,3},{3,2},{4,5},{5,4},{6,7},{7,6},{8,9},{9,8},{10,11... | collective-permute-start | bytes 4718600 | tf_op jit(solution)/shard_map/ppermute | solution.py:620
  130.6 9.8 %collective-permute-start.2 = (bf16[1536,384]{1,0:T(8,128)(2,1)}, bf16[1536,384]{1,0:T(8,128)(2,1)S(1)}, u32[]{:S(2)}, u32[]{:S(2)}) collective-permute-start(bf16[1536,384]{1,0:T(8,128)(2,1)} %get-tuple-element.34.out_own_ref), channel_id=1, source_target_pairs={{0,1},{1,0},{2,3},{3,2},{4,5},{5,4},{6,7},{7,6},{8,9},{9,8},{10,11... | collective-permute-start | bytes 3538952 | tf_op jit(solution)/shard_map/ppermute | solution.py:620
  132.5 30.6 %all-to-all-start.2 = ((bf16[16,64,384]{2,1,0:T(8,128)(2,1)}), bf16[16,64,384]{2,1,0:T(8,128)(2,1)S(1)}, u32[]{:S(2)}, u32[]{:S(2)}) async-start(bf16[16,64,384]{2,1,0:T(8,128)(2,1)} %bitcast.30), calls=%async_computation.2 | async-start | bytes 1572864 | tf_op jit(solution)/shard_map/all_to_all | solution.py:615
  140.4 1.4 copy-start.10
  141.9 0.9 copy-start.11
  154.2 3.3 %collective-permute-start.3 = (bf16[768,128]{1,0:T(8,128)(2,1)S(1)}, bf16[768,128]{1,0:T(8,128)(2,1)S(1)}, u32[]{:S(2)}, u32[]{:S(2)}) collective-permute-start(bf16[768,128]{1,0:T(8,128)(2,1)S(1)} %get-tuple-element.36), channel_id=1, source_target_pairs={{0,1},{1,0},{2,3},{3,2},{4,5},{5,4},{6,7},{7,6},{8,9},{9,8},{10,11... | collective-permute-start | bytes 589832 | tf_op jit(solution)/shard_map/ppermute | solution.py:620
  182.2 14.9 %all-to-all-start.4 = ((bf16[16,48,128]{2,1,0:T(8,128)(2,1)}), bf16[16,48,128]{2,1,0:T(8,128)(2,1)S(1)}, u32[]{:S(2)}, u32[]{:S(2)}) async-start(bf16[16,48,128]{2,1,0:T(8,128)(2,1)} %add_shards.1), calls=%async_computation.4 | async-start | bytes 393216 | tf_op jit(solution)/shard_map/all_to_all | solution.py:615
  186.9 1.1 copy-start.1
Sparse Core Ops, SparseCore 0:
  11.7 94.6 all-gather.1
where the time goes:
time: 206 us; the launch traced here: 205 us
  waiting for transfers between devices  82.6 us (40%)
  Pallas kernels  42.3 us (21%)
  starting transfers between devices  39.7 us (19%)
  blocking collectives  18.4 us (9%)
  between operations  14.2 us (7%)
  local copies, waits for them, and re-layouts  7.43 us (4%)
    all_to_all x4, waiting for transfers between devices, exchange(): return lax.all_to_all(data, axis, split_axis=0, concat_axis=0, tiled=True)  50.1 us
    all_to_all x4, starting transfers between devices, exchange(): return lax.all_to_all(data, axis, split_axis=0, concat_axis=0, tiled=True)  28.9 us
    all_gather x1, waiting for transfers between devices, on_device(): whole = lax.all_gather(shard, 'dp', axis=0, tiled=True)  27.7 us
    pallas_call x1, Pallas kernels, forward(): pl.pallas_call(forward_kernel, grid_spec=grid, out_shape=(jax.ShapeDtypeS...  19.3 us
    all_to_all x1, blocking collectives, exchange(): return lax.all_to_all(data, axis, split_axis=0, concat_axis=0, tiled=True)  18.4 us
    pallas_call x1, Pallas kernels, backward(): pl.pallas_call(backward_kernel, grid_spec=grid, out_shape=(jax.ShapeDtype...  11.3 us
    ppermute x4, starting transfers between devices, swap_cores(): return lax.ppermute(data, 'seq', pairs)  10.8 us
    unnamed x30, local copies, waits for them, and re-layouts  6.48 us
  transfers between devices with their start and end apart: 9, of which 6 were waited for; matrix products, arithmetic and copies ran while one was open for 0% of the time, Pallas kernels for 19%

commit v1 on v0

--- a/solution.py
+++ b/solution.py
@@ -496,7 +496,7 @@
             jax.ShapeDtypeStruct((HALF, 2 * RANK), F32),
         ),
         compiler_params=pltpu.CompilerParams(
-            vmem_limit_bytes=48 << 20, dimension_semantics=("arbitrary",)
+            vmem_limit_bytes=59 << 20, dimension_semantics=("arbitrary",)
         ),
         cost_estimate=pl.CostEstimate(flops=8 << 30, bytes_accessed=16 << 20, transcendentals=0),
         name="backward",

time: 206 us -> 207 us (level)
  waiting for transfers between devices: 82.6 us -> 79.9 us
  Pallas kernels: 42.3 us -> 44.4 us
    all_to_all x4, waiting for transfers between devices: 50.1 us -> 47.2 us  [exchange(): return lax.all_to_all(data, axis, split_axis=0, concat_axis=0, tiled=True)]
    pallas_call x1, Pallas kernels: 11.3 us -> 13.5 us  [backward(): pl.pallas_call(backward_kernel, grid_spec=grid, out_shape=(jax.ShapeDtype...]
  transfers between devices with their start and end apart: 9 -> 9, of which waited for: 6 -> 6; matrix products, arithmetic and copies ran while one was open for 0% -> 0% of each run, Pallas kernels for 19% -> 20%
where the time goes in v1:
time: 207 us; the launch traced here: 206 us
  waiting for transfers between devices  79.9 us (39%)
  Pallas kernels  44.4 us (21%)
  starting transfers between devices  41 us (20%)
  blocking collectives  18.4 us (9%)
  between operations  14.2 us (7%)
  local copies, waits for them, and re-layouts  8 us (4%)
    all_to_all x4, waiting for transfers between devices, exchange(): return lax.all_to_all(data, axis, split_axis=0, concat_axis=0, tiled=True)  47.2 us
    all_to_all x4, starting transfers between devices, exchange(): return lax.all_to_all(data, axis, split_axis=0, concat_axis=0, tiled=True)  30.4 us
    all_gather x1, waiting for transfers between devices, on_device(): whole = lax.all_gather(shard, 'dp', axis=0, tiled=True)  27.7 us
    pallas_call x1, Pallas kernels, forward(): pl.pallas_call(forward_kernel, grid_spec=grid, out_shape=(jax.ShapeDtypeS...  19.3 us
    all_to_all x1, blocking collectives, exchange(): return lax.all_to_all(data, axis, split_axis=0, concat_axis=0, tiled=True)  18.4 us
    pallas_call x1, Pallas kernels, backward(): pl.pallas_call(backward_kernel, grid_spec=grid, out_shape=(jax.ShapeDtype...  13.5 us
    ppermute x4, starting transfers between devices, swap_cores(): return lax.ppermute(data, 'seq', pairs)  10.6 us
    unnamed x30, local copies, waits for them, and re-layouts  7.06 us
  transfers between devices with their start and end apart: 9, of which 6 were waited for; matrix products, arithmetic and copies ran while one was open for 0% of the time, Pallas kernels for 20%

profile of v1, /device:TPU:1, one launch (start us, length us, event | category | flops | bytes accessed | tf_op | source)
XLA Modules:
  0.0 206.0 jit_solution(12519832749685315147)
XLA Ops:
  7.2 1.8 make_shard.1
  9.7 1.1 copy-done
  12.8 2.9 %pack.1 = bf16[16,32,1664]{2,1,0:T(8,128)(2,1)} custom-call(s32[16]{0:T(128)S(1)} %copy-done.5, s32[16]{0:T(128)S(1)} %copy-done.9, s32[16]{0:T(128)S(1)} %copy-done.7, bf16[256,1536]{1,0:T(8,128)(2,1)S(1)} %bitcast.18, f32[1,1536]{1,0:T(1,128)S(1)} %reshape.59.gain_ref), custom_call_target="tpu_custom_call" | custom-call | flops 402653184 | bytes 3145728 | tf_op jit(solution)/shard_map/pack/pallas_call | solution.py:84
  15.7 12.0 %all-to-all-start = ((bf16[16,32,1664]{2,1,0:T(8,128)(2,1)}), bf16[16,32,1664]{2,1,0:T(8,128)(2,1)S(1)}, u32[]{:S(2)}, u32[]{:S(2)}) async-start(bf16[16,32,1664]{2,1,0:T(8,128)(2,1)} %pack.1), calls=%async_computation | async-start | bytes 3407872 | tf_op jit(solution)/shard_map/all_to_all | solution.py:615
  27.7 2.4 %pack_masked.1 = bf16[16,32,1536]{2,1,0:T(8,128)(2,1)} custom-call(s32[16]{0:T(128)S(1)} %copy-done.6, s32[16]{0:T(128)S(1)} %copy-done.8, bf16[256,1536]{1,0:T(8,128)(2,1)S(1)} %bitcast.25), custom_call_target="tpu_custom_call" | custom-call | flops 402653184 | bytes 3145728 | tf_op jit(solution)/shard_map/pack_masked/pallas_call | solution.py:135
  30.1 38.6 %all-to-all-done = bf16[16,32,1664]{2,1,0:T(8,128)(2,1)S(1)} async-done(((bf16[16,32,1664]{2,1,0:T(8,128)(2,1)}), bf16[16,32,1664]{2,1,0:T(8,128)(2,1)S(1)}, u32[]{:S(2)}, u32[]{:S(2)}) %all-to-all-start) | async-done | bytes 1703968 | tf_op jit(solution)/shard_map/all_to_all | solution.py:615
  68.7 4.4 %all-to-all-start.1 = ((bf16[16,32,1536]{2,1,0:T(8,128)(2,1)}), bf16[16,32,1536]{2,1,0:T(8,128)(2,1)}, u32[]{:S(2)}, u32[]{:S(2)}) async-start(bf16[16,32,1536]{2,1,0:T(8,128)(2,1)} %pack_masked.1), calls=%async_computation.1 | async-start | bytes 3145728 | tf_op jit(solution)/shard_map/all_to_all | solution.py:615
  73.2 2.1 collective-permute-start
  75.3 3.4 %collective-permute-done = bf16[16,32,1664]{2,1,0:T(8,128)(2,1)S(1)} collective-permute-done((bf16[16,32,1664]{2,1,0:T(8,128)(2,1)S(1)}, bf16[16,32,1664]{2,1,0:T(8,128)(2,1)S(1)}, u32[]{:S(2)}, u32[]{:S(2)}) %collective-permute-start) | collective-permute-done | bytes 1703968 | tf_op jit(solution)/shard_map/ppermute | solution.py:620
  78.7 27.7 %all-gather.2.cloned.1.call-done.whole_ref = bf16[1536,1792]{1,0:T(8,128)(2,1)} async-done(((bf16[48,1792]{1,0:T(8,128)(2,1)}), bf16[1536,1792]{1,0:T(8,128)(2,1)}) %all-gather.2.cloned.1.call-update) | async-done | bytes 5505040 | tf_op jit(solution)/shard_map/all_gather | solution.py:640
  106.4 19.3 %forward.1 = (bf16[16,2,32,384]{3,2,1,0:T(8,128)(2,1)}, bf16[1536,384]{1,0:T(8,128)(2,1)}, bf16[2,4,512,512]{3,2,1,0:T(8,128)(2,1)}, bf16[2,1152,512]{2,1,0:T(8,...) custom-call(s32[1]{0:T(128)} %bitcast.core_ref, f32[8]{0:T(128)} %soft_ref.3, ...), custom_call_target="tpu_custom_call" | custom-call | flops 6442450944 | bytes 16777216 | tf_op jit(solution)/shard_map/forward/pallas_call | solution.py:303
  125.8 4.6 %collective-permute-start.1 = (bf16[16,32,1536]{2,1,0:T(8,128)(2,1)}, bf16[16,32,1536]{2,1,0:T(8,128)(2,1)}, u32[]{:S(2)}, u32[]{:S(2)}) collective-permute-start(bf16[16,32,1536]{2,1,0:T(8,128)(2,1)} %all-to-all-done.1), channel_id=1, source_target_pairs={{0,1},{1,0},{2,3},{3,2},{4,5},{5,4},{6,7},{7,6},{8,9},{9,8},{10,11... | collective-permute-start | bytes 4718600 | tf_op jit(solution)/shard_map/ppermute | solution.py:620
  130.4 1.9 collective-permute-start.2
  132.3 7.9 %all-to-all-start.2 = ((bf16[16,64,384]{2,1,0:T(8,128)(2,1)}), bf16[16,64,384]{2,1,0:T(8,128)(2,1)S(1)}, u32[]{:S(2)}, u32[]{:S(2)}) async-start(bf16[16,64,384]{2,1,0:T(8,128)(2,1)} %bitcast.30), calls=%async_computation.2 | async-start | bytes 1572864 | tf_op jit(solution)/shard_map/all_to_all | solution.py:615
  140.3 1.0 copy-done.12
  141.3 13.5 %backward.1 = (f32[768,128]{1,0:T(8,128)}, bf16[768,128]{1,0:T(8,128)(2,1)}, f32[384,128]{1,0:T(8,128)}) custom-call(s32[1]{0:T(128)} %bitcast.core_ref, f32[8]{0:T(128)} %soft_ref.3, bf16[2,4,512,512]{3,2,1,0:T(8,128)(2,1)} %get-tuple-element.26.weights_ref, bf16[2,1152,512]{2,1,0:T(8,128)(2,1)} %get-tuple-element.27.qkv_ref, ...), custom_call_target="tpu_custom_call" | custom-call | flops 8589934592 | bytes 16777216 | tf_op jit(solution)/shard_map/backward/pallas_call | solution.py:490
  154.8 2.0 collective-permute-start.3
  156.8 1.5 collective-permute-done.3.come_ref
  158.3 1.0 copy-done.3
  160.3 2.6 %all-to-all-done.2.context_ref = bf16[16,64,384]{2,1,0:T(8,128)(2,1)S(1)} async-done(((bf16[16,64,384]{2,1,0:T(8,128)(2,1)}), bf16[16,64,384]{2,1,0:T(8,128)(2,1)S(1)}, u32[]{:S(2)}, u32[]{:S(2)}) %all-to-all-start.2) | async-done | bytes 786464 | tf_op jit(solution)/shard_map/all_to_all | solution.py:615
  162.9 18.4 %all_to_all.25.part_ref = bf16[32,48,128]{2,1,0:T(8,128)(2,1)S(1)} all-to-all(bf16[32,48,128]{2,1,0:T(8,128)(2,1)S(1)} %bitcast.24), channel_id=1, replica_groups=mesh['dp'=32,'seq'=16] {'dp'}, dimensions={0} | all-to-all | bytes 786432 | tf_op jit(solution)/shard_map/all_to_all | solution.py:615
  182.0 6.1 %all-to-all-start.4 = ((bf16[16,48,128]{2,1,0:T(8,128)(2,1)}), bf16[16,48,128]{2,1,0:T(8,128)(2,1)S(1)}, u32[]{:S(2)}, u32[]{:S(2)}) async-start(bf16[16,48,128]{2,1,0:T(8,128)(2,1)} %add_shards.1), calls=%async_computation.4 | async-start | bytes 393216 | tf_op jit(solution)/shard_map/all_to_all | solution.py:615
  189.4 3.1 %finish.1 = bf16[256,1536]{1,0:T(8,128)(2,1)} custom-call(s32[1]{0:T(128)} %bitcast.core_ref, s32[16]{0:T(128)S(1)} %copy-done.6, s32[16]{0:T(128)S(1)} %copy-done.8, bf16[16,64,384]{2,1,0:T(8,128)(2,1)S(1)} %all-to-all-done.2.context_ref, bf16[256,1536]{1,0:T(8,128)(2,1)S(1)} %bitcast.19, bf16[768,384]{1,0:T(8,128)(2,1)S(1)} %bitcast.21, ...), custom_call_target="tpu_custom_call" | custom-call | flops 805306368 | bytes 6291456 | tf_op jit(solution)/shard_map/finish/pallas_call | solution.py:554
  192.4 6.0 %all-to-all-done.4.part_ref = bf16[16,48,128]{2,1,0:T(8,128)(2,1)S(1)} async-done(((bf16[16,48,128]{2,1,0:T(8,128)(2,1)}), bf16[16,48,128]{2,1,0:T(8,128)(2,1)S(1)}, u32[]{:S(2)}, u32[]{:S(2)}) %all-to-all-start.4) | async-done | bytes 196640 | tf_op jit(solution)/shard_map/all_to_all | solution.py:615
  (38 shorter events, 6.4 us)
Async XLA Ops:
  7.2 99.2 %all-gather.2.cloned.1.call-start = ((), (), s32[]{:S(2)}) async-start(), calls=%async_computation.5 | async-start | bytes 5677056 | tf_op jit(solution)/shard_map/all_gather | solution.py:640
  9.7 1.1 copy-start
  10.9 0.7 copy-start.5
  11.5 0.7 copy-start.7
  12.2 0.7 copy-start.9
  15.7 12.0 %copy-start.2 = (bf16[16,16,1536]{2,1,0:T(8,128)(2,1)S(1)}, bf16[16,16,1536]{2,1,0:T(8,128)(2,1)}, u32[]{:S(2)}) copy-start(bf16[16,16,1536]{2,1,0:T(8,128)(2,1)} %param.21) | copy-start | bytes 2359300
  15.7 12.0 %copy-start.6 = (s32[16]{0:T(128)S(1)}, s32[16]{0:T(128)}, u32[]{:S(2)}) copy-start(s32[16]{0:T(128)} %owner_ref.5) | copy-start | bytes 196
  15.7 12.0 %copy-start.8 = (s32[16]{0:T(128)S(1)}, s32[16]{0:T(128)}, u32[]{:S(2)}) copy-start(s32[16]{0:T(128)} %live_ref.5) | copy-start | bytes 196
  15.7 53.0 %all-to-all-start = ((bf16[16,32,1664]{2,1,0:T(8,128)(2,1)}), bf16[16,32,1664]{2,1,0:T(8,128)(2,1)S(1)}, u32[]{:S(2)}, u32[]{:S(2)}) async-start(bf16[16,32,1664]{2,1,0:T(8,128)(2,1)} %pack.1), calls=%async_computation | async-start | bytes 3407872 | tf_op jit(solution)/shard_map/all_to_all | solution.py:615
  68.7 4.4 %copy-start.10 = (bf16[16,32,1664]{2,1,0:T(8,128)(2,1)}, bf16[16,32,1664]{2,1,0:T(8,128)(2,1)S(1)}, u32[]{:S(2)}) copy-start(bf16[16,32,1664]{2,1,0:T(8,128)(2,1)S(1)} %all-to-all-done) | copy-start | bytes 5111812
  68.7 57.0 %all-to-all-start.1 = ((bf16[16,32,1536]{2,1,0:T(8,128)(2,1)}), bf16[16,32,1536]{2,1,0:T(8,128)(2,1)}, u32[]{:S(2)}, u32[]{:S(2)}) async-start(bf16[16,32,1536]{2,1,0:T(8,128)(2,1)} %pack_masked.1), calls=%async_computation.1 | async-start | bytes 3145728 | tf_op jit(solution)/shard_map/all_to_all | solution.py:615
  73.2 5.5 %collective-permute-start = (bf16[16,32,1664]{2,1,0:T(8,128)(2,1)S(1)}, bf16[16,32,1664]{2,1,0:T(8,128)(2,1)S(1)}, u32[]{:S(2)}, u32[]{:S(2)}) collective-permute-start(bf16[16,32,1664]{2,1,0:T(8,128)(2,1)S(1)} %all-to-all-done), channel_id=1, source_target_pairs={{0,1},{1,0},{2,3},{3,2},{4,5},{5,4},{6,7},{7,6},{8,9},{9,8},{10,11... | collective-permute-start | bytes 5111816 | tf_op jit(solution)/shard_map/ppermute | solution.py:620
  78.7 27.7 %copy-start.14 = (bf16[16,32,1664]{2,1,0:T(8,128)(2,1)}, bf16[16,32,1664]{2,1,0:T(8,128)(2,1)S(1)}, u32[]{:S(2)}) copy-start(bf16[16,32,1664]{2,1,0:T(8,128)(2,1)S(1)} %collective-permute-done) | copy-start | bytes 5111812
  125.8 14.5 %collective-permute-start.1 = (bf16[16,32,1536]{2,1,0:T(8,128)(2,1)}, bf16[16,32,1536]{2,1,0:T(8,128)(2,1)}, u32[]{:S(2)}, u32[]{:S(2)}) collective-permute-start(bf16[16,32,1536]{2,1,0:T(8,128)(2,1)} %all-to-all-done.1), channel_id=1, source_target_pairs={{0,1},{1,0},{2,3},{3,2},{4,5},{5,4},{6,7},{7,6},{8,9},{9,8},{10,11... | collective-permute-start | bytes 4718600 | tf_op jit(solution)/shard_map/ppermute | solution.py:620
  130.4 9.8 %collective-permute-start.2 = (bf16[1536,384]{1,0:T(8,128)(2,1)}, bf16[1536,384]{1,0:T(8,128)(2,1)S(1)}, u32[]{:S(2)}, u32[]{:S(2)}) collective-permute-start(bf16[1536,384]{1,0:T(8,128)(2,1)} %get-tuple-element.34.out_own_ref), channel_id=1, source_target_pairs={{0,1},{1,0},{2,3},{3,2},{4,5},{5,4},{6,7},{7,6},{8,9},{9,8},{10,11... | collective-permute-start | bytes 3538952 | tf_op jit(solution)/shard_map/ppermute | solution.py:620
  132.3 30.6 %all-to-all-start.2 = ((bf16[16,64,384]{2,1,0:T(8,128)(2,1)}), bf16[16,64,384]{2,1,0:T(8,128)(2,1)S(1)}, u32[]{:S(2)}, u32[]{:S(2)}) async-start(bf16[16,64,384]{2,1,0:T(8,128)(2,1)} %bitcast.30), calls=%async_computation.2 | async-start | bytes 1572864 | tf_op jit(solution)/shard_map/all_to_all | solution.py:615
  140.2 1.0 copy-start.12
  141.3 46.8 %copy-start.11 = (bf16[1536,384]{1,0:T(8,128)(2,1)S(1)}, bf16[1536,384]{1,0:T(8,128)(2,1)}, u32[]{:S(2)}) copy-start(bf16[1536,384]{1,0:T(8,128)(2,1)} %get-tuple-element.34.out_own_ref) | copy-start | bytes 3538948
  154.8 3.5 %collective-permute-start.3 = (bf16[768,128]{1,0:T(8,128)(2,1)}, bf16[768,128]{1,0:T(8,128)(2,1)S(1)}, u32[]{:S(2)}, u32[]{:S(2)}) collective-permute-start(bf16[768,128]{1,0:T(8,128)(2,1)} %get-tuple-element.36), channel_id=1, source_target_pairs={{0,1},{1,0},{2,3},{3,2},{4,5},{5,4},{6,7},{7,6},{8,9},{9,8},{10,11... | collective-permute-start | bytes 589832 | tf_op jit(solution)/shard_map/ppermute | solution.py:620
  158.3 1.0 copy-start.3
  159.3 0.9 copy-start.4
  181.3 7.0 %copy-start.13 = (bf16[1536,384]{1,0:T(8,128)(2,1)S(1)}, bf16[1536,384]{1,0:T(8,128)(2,1)}, u32[]{:S(2)}) copy-start(bf16[1536,384]{1,0:T(8,128)(2,1)} %copy-done.12) | copy-start | bytes 3538948
  182.0 16.4 %all-to-all-start.4 = ((bf16[16,48,128]{2,1,0:T(8,128)(2,1)}), bf16[16,48,128]{2,1,0:T(8,128)(2,1)S(1)}, u32[]{:S(2)}, u32[]{:S(2)}) async-start(bf16[16,48,128]{2,1,0:T(8,128)(2,1)} %add_shards.1), calls=%async_computation.4 | async-start | bytes 393216 | tf_op jit(solution)/shard_map/all_to_all | solution.py:615
  188.2 1.1 copy-start.1
Sparse Core Ops, SparseCore 0:
  11.7 94.6 all-gather.1
